TPU v7x, 256 devices: a whole 4x4x8 slice. The times are simulated.
256 devices in a mesh: gy: 32 (over z_hi, y, x), gz: 8 (over z_lo, core).
Axes of the slice: x: 4, y: 4, z: 8 (z_hi: 2, z_lo: 4; z = z_hi * 4 + z_lo), core: 2. Of those that a mesh axis runs over, the one named last changes fastest.
Arguments:
- kspace: float32 [2, 4, 256, 32, 256], P(None, None, 'gy', 'gz'), may hold values from -6 to 6
- cotangent: float32 [2, 4, 256, 32, 256], P(None, None, 'gy', 'gz'), may hold values from -6 to 6
- weight_in: bfloat16 [16, 8, 3, 3, 3], replicated, may hold values from -0.4375 to 0.4375
- weight_out: bfloat16 [8, 16, 3, 3, 3], replicated, may hold values from -0.3125 to 0.3125
- consistency_weight: float32 [1], replicated, may hold values from 0.2 to 1
- sampling_mask: int32 [256, 32], P('gy', 'gz'), may hold values 0 or 1
Outputs:
- grad_kspace: float32 [2, 4, 256, 32, 256], P(None, None, 'gy', 'gz')
- grad_weight_in: float32 [16, 8, 3, 3, 3], replicated
- grad_weight_out: float32 [8, 16, 3, 3, 3], replicated
Inputs may be any that keep to these rules, and one draw needn't show every extreme that they name: `sampling_mask`: 1 marks a sampled phase-encode line.
All inputs are finite; a program needn't handle non-finite values. No bound on the sum of `sampling_mask` on one device may be relied on, other than what follows from the above.
Results may differ from a plain program's by a relative error of at most 0.0059.
Values may be sent and summed in bfloat16 or wider, within the bound.
A program may use at most 128 MiB of HBM per device.

v0:
```python
import math
import jax
import jax.numpy as jnp
from jax import lax
from jax.sharding import PartitionSpec as P


def as_sent(shard):
    return jax.tree.map(lambda a: a.astype(jnp.bfloat16) if a.dtype == jnp.float32 else a, shard)


def extended(shard, sides, width):
    for axis, dim in sides:
        count, length = (lax.axis_size(axis), shard.shape[dim])
        up = [(i, (i + 1) % count) for i in range(count - 1)]
        down = [(j, i) for i, j in up]
        last = lax.slice_in_dim(shard, length - width, length, axis=dim)
        first = lax.slice_in_dim(shard, 0, width, axis=dim)
        before = lax.ppermute(last, axis, up)
        after = lax.ppermute(first, axis, down)
        shard = jnp.concatenate([before, shard, after], axis=dim)
    return shard


def dft_table(length, direction):
    indices = lax.iota(jnp.int32, length)
    products = indices[:, None] * indices[None, :] % length
    phases = products.astype(jnp.float32) * (2.0 * math.pi / length)
    cosine = jnp.cos(phases) / math.sqrt(length)
    sine_part = direction * jnp.sin(phases) / math.sqrt(length)
    return jnp.stack([jnp.stack([cosine, -sine_part]), jnp.stack([sine_part, cosine])])


def spectral(spectrum, direction):
    field_parts = spectrum.shape[1]
    cells_y = spectrum.shape[2]
    cells_z = spectrum.shape[3]
    readout = spectrum.shape[4]
    length_y = cells_y * lax.axis_size("gy")
    length_z = cells_z * lax.axis_size("gz")
    table_y = dft_table(length_y, direction)
    table_z = dft_table(length_z, direction)
    flattened = spectrum.reshape(2, field_parts, cells_y, cells_z * readout)
    transformed_y = jnp.einsum(
        "pqvy,qcym->pcvm",
        table_y,
        lax.all_to_all(flattened, "gy", split_axis=3, concat_axis=2, tiled=True),
        precision=lax.Precision.HIGHEST,
    )
    turned_field = lax.all_to_all(
        lax.all_to_all(transformed_y, "gy", split_axis=2, concat_axis=3, tiled=True),
        "gz",
        split_axis=2,
        concat_axis=3,
        tiled=True,
    )
    shaped = turned_field.reshape(
        turned_field.shape[0], turned_field.shape[1], turned_field.shape[2], length_z, readout
    )
    turned = jnp.einsum("pqwz,qcyzx->pcywx", table_z, shaped, precision=lax.Precision.HIGHEST)
    transformed_z = turned.reshape(turned_field.shape)
    result = lax.all_to_all(
        as_sent(transformed_z), "gz", split_axis=3, concat_axis=2, tiled=True
    ).astype(transformed_z.dtype)
    return result.reshape(spectrum.shape)


def with_rims(volume):
    return extended(volume, (("gy", 2), ("gz", 3)), 1)


def convolve(padded, kernel):
    return lax.conv_general_dilated(
        padded,
        kernel,
        (1, 1, 1),
        ((0, 0), (0, 0), (1, 1)),
        dimension_numbers=("NCDHW", "OIDHW", "NCDHW"),
        preferred_element_type=jnp.float32,
    )


def kernel_gradient(padded, cotangent_part):
    summed = lax.conv_general_dilated(
        padded,
        cotangent_part,
        (1, 1, 1),
        ((0, 0), (0, 0), (1, 1)),
        dimension_numbers=("CNDHW", "IODHW", "NCDHW"),
        preferred_element_type=jnp.float32,
    )
    return summed.transpose(1, 0, 2, 3, 4)


def flipped(kernel):
    return jnp.flip(kernel, (2, 3, 4)).transpose(1, 0, 2, 3, 4)


def local(kspace, cotangent, weight_in, weight_out, consistency_weight, sampling_mask):
    coil_count = kspace.shape[1]
    channels = 2 * coil_count
    cells_y = kspace.shape[2]
    cells_z = kspace.shape[3]
    readout = kspace.shape[4]
    voxels = readout * cells_y * cells_z * lax.axis_size("gy") * lax.axis_size("gz")
    image_field = spectral(kspace, 1.0)
    back_field = spectral(cotangent, 1.0)
    image_in = image_field.astype(jnp.bfloat16).reshape(1, channels, cells_y, cells_z, readout)
    back_out = (-back_field).astype(jnp.bfloat16).reshape(1, channels, cells_y, cells_z, readout)
    image_padded = with_rims(image_in)
    back_padded = with_rims(back_out)
    hidden = convolve(image_padded, weight_in)
    active = jax.nn.silu(hidden).astype(jnp.bfloat16)
    active_padded = with_rims(active)
    local_out = kernel_gradient(active_padded, back_out)
    back_active = convolve(back_padded, flipped(weight_out))
    gate = jax.nn.sigmoid(hidden)
    back_hidden = (back_active * gate * (1.0 + hidden * (1.0 - gate))).astype(jnp.bfloat16)
    local_in = kernel_gradient(image_padded, back_hidden)
    hidden_padded = with_rims(back_hidden)
    back_image = convolve(hidden_padded, flipped(weight_in))
    spectrum = spectral(back_image.reshape(2, coil_count, cells_y, cells_z, readout), -1.0)
    summed_in, summed_out = lax.psum((local_in, local_out), ("gy", "gz"))
    scale = 1.0 / math.sqrt(voxels)
    mask_field = sampling_mask.astype(jnp.float32)[None, None, :, :, None]
    grad_kspace = cotangent - consistency_weight[0] * mask_field * cotangent + spectrum
    return (grad_kspace, summed_in * scale, summed_out * scale)


def solution(mesh):
    placed = (
        P(None, None, "gy", "gz", None),
        P(None, None, "gy", "gz", None),
        P(),
        P(),
        P(),
        P("gy", "gz"),
    )
    return jax.shard_map(
        local,
        mesh=mesh,
        in_specs=placed,
        out_specs=(P(None, None, "gy", "gz", None), P(), P()),
        check_vma=False,
    )
```

profile of v0, /device:TPU:1, one launch (start us, length us, event | category | flops | bytes accessed | tf_op | source)
XLA Modules:
  0.0 722.7 jit_solution(2760864033944492216)
XLA Ops:
  0.7 4.5 copy.348
  5.2 6.9 reshape.431
  12.1 14.5 %all-to-all-start.4 = ((f32[32,1,2048]{2,1,0:T(1,128)}), f32[32,1,2048]{2,1,0:T(1,128)S(1)}, u32[]{:S(2)}, u32[]{:S(2)}) async-start(f32[32,1,2048]{2,1,0:T(1,128)} %reshape.431), calls=%async_computation.4 | async-start | bytes 524288 | tf_op jit(solution)/shard_map/all_to_all | solution.py:47
  29.7 6.9 reshape.437
  38.5 11.0 %all-to-all-start = ((f32[32,1,2048]{2,1,0:T(1,128)}), f32[32,1,2048]{2,1,0:T(1,128)S(1)}, u32[]{:S(2)}, u32[]{:S(2)}) async-start(f32[32,1,2048]{2,1,0:T(1,128)} %reshape.437), calls=%async_computation | async-start | bytes 524288 | tf_op jit(solution)/shard_map/all_to_all | solution.py:47
  54.6 6.3 reshape.432
  60.9 3.5 copy.417
  68.4 12.0 %all-to-all-start.5 = ((f32[32,1,2048]{2,1,0:T(1,128)}), f32[32,1,2048]{2,1,0:T(1,128)S(1)}, u32[]{:S(2)}, u32[]{:S(2)}) async-start(f32[32,1,2048]{2,1,0:T(1,128)} %reshape.433), calls=%async_computation.5 | async-start | bytes 524288 | tf_op jit(solution)/shard_map/all_to_all | solution.py:51
  81.7 6.3 reshape.438
  88.0 3.5 copy.411
  95.5 11.8 %all-to-all-start.1 = ((f32[32,1,2048]{2,1,0:T(1,128)}), f32[32,1,2048]{2,1,0:T(1,128)S(1)}, u32[]{:S(2)}, u32[]{:S(2)}) async-start(f32[32,1,2048]{2,1,0:T(1,128)} %reshape.439), calls=%async_computation.1 | async-start | bytes 524288 | tf_op jit(solution)/shard_map/all_to_all | solution.py:51
  110.7 8.5 %all-to-all-done.1 = f32[32,1,2048]{2,1,0:T(1,128)S(1)} async-done(((f32[32,1,2048]{2,1,0:T(1,128)}), f32[32,1,2048]{2,1,0:T(1,128)S(1)}, u32[]{:S(2)}, u32[]{:S(2)}) %all-to-all-start.1) | async-done | bytes 262176 | tf_op jit(solution)/shard_map/all_to_all | solution.py:51
  119.2 7.4 %all-to-all-start.6 = ((f32[2,4,8,1024]{3,1,0,2:T(4,128)}), f32[2,4,8,1024]{3,1,0,2:T(4,128)S(1)}, u32[]{:S(2)}, u32[]{:S(2)}) async-start(f32[2,4,8,1024]{3,1,0,2:T(4,128)} %reshape.424), calls=%async_computation.6 | async-start | bytes 524288 | tf_op jit(solution)/shard_map/all_to_all | solution.py:50
  130.3 5.1 all-to-all-done.6
  135.4 4.8 all-to-all-start.2
  141.7 5.0 copy.421
  146.6 9.3 %reshape.435 = bf16[8,2,4096]{2,1,0:T(2,128)(2,1)} reshape(bf16[8192,1,2,4]{3,2,1,0:T(2,128)(2,1)} %bitcast.299) | data formatting | bytes 262144
  156.0 5.1 all-to-all-start.7
  162.4 5.0 copy.415
  167.4 9.3 %reshape.441 = bf16[8,2,4096]{2,1,0:T(2,128)(2,1)} reshape(bf16[8192,1,2,4]{3,2,1,0:T(2,128)(2,1)} %bitcast.300) | data formatting | bytes 262144
  176.7 5.1 all-to-all-start.3
  182.5 10.0 %reshape.436 = bf16[8192,1,2,4]{3,2,1,0:T(2,128)(2,1)} reshape(bf16[8,2,4096]{2,1,0:T(2,128)(2,1)S(1)} %all-to-all-done.7) | data formatting | bytes 262144
  192.6 8.6 %copy.358 = bf16[2,4,1,8192]{3,1,0,2:T(4,128)(2,1)S(1)} copy(bf16[2,4,1,8192]{1,0,2,3:T(2,128)(2,1)} %bitcast.301) | data formatting | bytes 262144 | tf_op jit(solution)/shard_map/all_to_all | solution.py:62
  203.3 10.1 %reshape.442 = bf16[8192,1,2,4]{3,2,1,0:T(2,128)(2,1)} reshape(bf16[8,2,4096]{2,1,0:T(2,128)(2,1)S(1)} %all-to-all-done.3) | data formatting | bytes 262144
  213.4 8.6 %copy.344 = bf16[2,4,1,8192]{3,1,2,0:T(4,128)(2,1)S(1)} copy(bf16[2,4,1,8192]{1,0,2,3:T(2,128)(2,1)} %bitcast.302) | data formatting | bytes 262144 | tf_op jit(solution)/shard_map/all_to_all | solution.py:62
  222.2 7.4 %copy.396 = bf16[1,8,8,4,256]{1,0,4,3,2:T(2,128)(2,1)} copy(bf16[1,8,8,4,256]{4,3,2,1,0:T(4,128)(2,1)S(1)} %convert_element_type.199) | data formatting | bytes 262144 | tf_op jit(solution)/shard_map/convert_element_type | solution.py:109
  230.9 4.0 collective-permute-start
  236.5 4.4 collective-permute-start.6
  243.7 3.6 collective-permute-start.2
  254.5 4.8 copy.361
  263.3 4.6 copy.347
  269.0 9.1 %multiply_convert_fusion.1 = (bf16[8,4,8,33,16]{4,2,3,1,0:T(8,128)(2,1)}, f32[8,4,8,33,16]{4,2,3,1,0:T(8,128)S(1)}) fusion(pred[8,33]{0,1:T(8,128)(4,1)S(1)} %copy-done.15, bf16[16,8,3,3,3]{0,1,4,3,2:T(8,128)(2,1)S(1)} %copy-done, bf16[8,10,6,1,7,2]{0,4,5,2,1,3:T(8,128)(2,1)S(1)} %copy-done.8, bf16[8,10,6,1,8,33]{0,4,5,2,1,3:T(8,128)(2,1)} %copy.361), kind=kOutput, calls=%fused_computation.16 | convolution fusion | flops 60009984 | bytes 1085064 | tf_op jit(solution)/shard_map/conv_general_dilated | solution.py:73
  278.2 9.5 %multiply_convert_fusion = bf16[8,4,8,33,16]{4,2,3,1,0:T(8,128)(2,1)} fusion(f32[8,4,8,33,16]{4,2,3,1,0:T(8,128)S(1)} %get-tuple-element.36, bf16[8,16,3,3,3]{1,0,4,3,2:T(8,128)(2,1)S(1)} %copy-done.14, bf16[8,10,6,1,7,2]{0,4,5,2,1,3:T(8,128)(2,1)S(1)} %slice.86, bf16[8,10,6,1,8,33]{0,4,5,2,1,3:T(8,128)(2,1)S(1)} %copy-done.2, pred[8,33]{0,1:T(8,128)(4,1)S(1)} %copy-done.15), kind=kOutput, calls=%fused_computation.15 | convolution fusion | flops 60685824 | bytes 1085064 | tf_op jit(solution)/shard_map/conv_general_dilated | solution.py:73
  287.7 3.7 copy.363
  296.9 5.2 collective-permute-start.12
  306.7 4.0 collective-permute-start.8
  312.5 4.8 copy.442
  320.3 4.5 collective-permute-start.10
  326.7 4.0 fusion.33
  330.7 3.5 copy.441
  340.1 4.7 copy.368
  345.9 9.1 %broadcast_select_fusion = f32[8,4,8,33,8]{4,2,3,1,0:T(8,128)} fusion(pred[8,33]{0,1:T(8,128)(4,1)S(1)} %copy-done.15, bf16[16,8,3,3,3]{0,1,4,3,2:T(8,128)(2,1)S(1)} %copy-done, bf16[16,10,6,1,7,2]{0,4,5,2,1,3:T(8,128)(2,1)S(1)} %slice.97, bf16[16,10,6,1,8,33]{0,4,5,2,1,3:T(8,128)(2,1)} %copy.368), kind=kOutput, calls=%fused_computation.41 | convolution fusion | flops 60072960 | bytes 811272 | tf_op jit(solution)/shard_map/conv_general_dilated | solution.py:73
  355.0 3.5 copy.369
  361.5 6.9 reshape.443
  368.4 37.0 %all-to-all-start.8 = ((f32[32,1,2048]{2,1,0:T(1,128)}), f32[32,1,2048]{2,1,0:T(1,128)S(1)}, u32[]{:S(2)}, u32[]{:S(2)}) async-start(f32[32,1,2048]{2,1,0:T(1,128)} %reshape.443), calls=%async_computation.8 | async-start | bytes 524288 | tf_op jit(solution)/shard_map/all_to_all | solution.py:47
  405.4 3.9 fusion.35
  409.3 3.7 copy.391
  414.7 4.5 copy.388
  420.6 3.9 collective-permute-start.14
  427.8 6.4 reshape.444
  434.2 3.7 copy.436
  437.8 5.4 convolution_bitcast_fusion.5
  446.6 12.3 %all-to-all-start.9 = ((f32[32,1,2048]{2,1,0:T(1,128)}), f32[32,1,2048]{2,1,0:T(1,128)S(1)}, u32[]{:S(2)}, u32[]{:S(2)}) async-start(f32[32,1,2048]{2,1,0:T(1,128)} %reshape.445), calls=%async_computation.9 | async-start | bytes 524288 | tf_op jit(solution)/shard_map/all_to_all | solution.py:51
  458.9 22.9 %fusion.52 = f32[16,8,3,3,3]{0,1,4,3,2:T(8,128)} fusion(bf16[8,4,8,33,16]{4,2,3,1,0:T(8,128)(2,1)S(1)} %copy-done.5, pred[8,33]{0,1:T(8,128)(4,1)S(1)} %copy-done.15, bf16[8,10,6,8,33,1]{3,0,5,4,2,1:T(8,128)(2,1)} %fusion.33, bf16[8,10,6,8,33,1]{3,0,5,4,2,1:T(8,128)(2,1)} %copy.388, bf16[8,10,6,8,33,1]{3,0,5,4,2,1:T(8,128)(2,1)} %fusion.35), kind=kOutput, calls=%fused_computation.59 | convolution fusion | flops 59288064 | bytes 1044744 | tf_op jit(solution)/shard_map/transpose | solution.py:92
  482.8 12.0 %copy.395 = bf16[1,16,10,6,256]{1,0,4,3,2:T(2,128)(2,1)} copy(bf16[1,16,10,6,256]{4,1,3,2,0:T(8,128)(2,1)S(1)} %pad_maximum_fusion.7) | data formatting | bytes 983040 | tf_op jit(solution)/shard_map/concatenate | solution.py:21
  498.6 5.5 all-to-all-start.10
  504.1 90.1 %fusion.123 = f32[8,16,3,3,3]{1,0,4,3,2:T(8,128)S(1)} fusion(bf16[1,16,10,6,256]{1,0,4,3,2:T(2,128)(2,1)} %copy.395, bf16[1,8,8,4,256]{1,0,4,3,2:T(2,128)(2,1)} %copy.396), kind=kOutput, calls=%fused_computation.182 | convolution fusion | flops 56475648 | bytes 636416 | tf_op jit(solution)/shard_map/transpose | solution.py:92
  594.2 82.3 %all-reduce = (f32[16,8,3,3,3]{0,1,4,3,2:T(8,128)S(1)}, f32[8,16,3,3,3]{1,0,4,3,2:T(8,128)S(1)}) all-reduce(f32[16,8,3,3,3]{0,1,4,3,2:T(8,128)S(1)} %copy-done.11, f32[8,16,3,3,3]{1,0,4,3,2:T(8,128)S(1)} %fusion.123), channel_id=1, replica_groups=mesh['gy'=32,'gz'=8] {'gy','gz'}, use_global_device_ids=true, to_apply=%region_0.1 | all-reduce | flops 6912 | bytes 55296 | tf_op jit(solution)/shard_map/psum | solution.py:123
  677.9 5.0 copy.428
  682.8 9.3 %reshape.447 = bf16[8,2,4096]{2,1,0:T(2,128)(2,1)} reshape(bf16[8192,1,2,4]{3,2,1,0:T(2,128)(2,1)} %bitcast.304) | data formatting | bytes 262144
  692.1 4.0 all-to-all-start.11
  696.8 5.2 all-to-all-done.11
  701.9 10.0 %reshape.448 = bf16[8192,1,2,4]{3,2,1,0:T(2,128)(2,1)} reshape(bf16[8,2,4096]{2,1,0:T(2,128)(2,1)S(1)} %all-to-all-done.11) | data formatting | bytes 262144
  712.0 9.6 %copy.381 = f32[2,4,8,4,256]{4,3,2,1,0:T(4,128)S(1)} copy(bf16[2,4,8,4,256]{1,0,4,3,2:T(2,128)(2,1)} %bitcast.305) | data formatting | bytes 393216 | tf_op jit(solution)/shard_map/convert_element_type | solution.py:64
  (172 shorter events, 93.0 us)
Async XLA Ops:
  0.6 268.4 %copy-start = (bf16[16,8,3,3,3]{0,1,4,3,2:T(8,128)(2,1)S(1)}, bf16[16,8,3,3,3]{0,1,4,3,2:T(8,128)(2,1)}, u32[]{:S(2)}) copy-start(bf16[16,8,3,3,3]{0,1,4,3,2:T(8,128)(2,1)} %param.8) | copy-start | bytes 20740
  0.6 25.9 %copy-start.6 = (f32[2,4,8,4,256]{4,3,2,1,0:T(4,128)S(1)}, f32[2,4,8,4,256]{4,3,2,1,0:T(4,128)}, u32[]{:S(2)}) copy-start(f32[2,4,8,4,256]{4,3,2,1,0:T(4,128)} %param.7) | copy-start | bytes 786436
  12.1 26.5 %all-to-all-start.4 = ((f32[32,1,2048]{2,1,0:T(1,128)}), f32[32,1,2048]{2,1,0:T(1,128)S(1)}, u32[]{:S(2)}, u32[]{:S(2)}) async-start(f32[32,1,2048]{2,1,0:T(1,128)} %reshape.431), calls=%async_computation.4 | async-start | bytes 524288 | tf_op jit(solution)/shard_map/all_to_all | solution.py:47
  38.5 29.9 %all-to-all-start = ((f32[32,1,2048]{2,1,0:T(1,128)}), f32[32,1,2048]{2,1,0:T(1,128)S(1)}, u32[]{:S(2)}, u32[]{:S(2)}) async-start(f32[32,1,2048]{2,1,0:T(1,128)} %reshape.437), calls=%async_computation | async-start | bytes 524288 | tf_op jit(solution)/shard_map/all_to_all | solution.py:47
  68.4 27.1 %all-to-all-start.5 = ((f32[32,1,2048]{2,1,0:T(1,128)}), f32[32,1,2048]{2,1,0:T(1,128)S(1)}, u32[]{:S(2)}, u32[]{:S(2)}) async-start(f32[32,1,2048]{2,1,0:T(1,128)} %reshape.433), calls=%async_computation.5 | async-start | bytes 524288 | tf_op jit(solution)/shard_map/all_to_all | solution.py:51
  95.5 23.8 %all-to-all-start.1 = ((f32[32,1,2048]{2,1,0:T(1,128)}), f32[32,1,2048]{2,1,0:T(1,128)S(1)}, u32[]{:S(2)}, u32[]{:S(2)}) async-start(f32[32,1,2048]{2,1,0:T(1,128)} %reshape.439), calls=%async_computation.1 | async-start | bytes 524288 | tf_op jit(solution)/shard_map/all_to_all | solution.py:51
  119.2 16.2 %all-to-all-start.6 = ((f32[2,4,8,1024]{3,1,0,2:T(4,128)}), f32[2,4,8,1024]{3,1,0,2:T(4,128)S(1)}, u32[]{:S(2)}, u32[]{:S(2)}) async-start(f32[2,4,8,1024]{3,1,0,2:T(4,128)} %reshape.424), calls=%async_computation.6 | async-start | bytes 524288 | tf_op jit(solution)/shard_map/all_to_all | solution.py:50
  135.4 20.6 %all-to-all-start.2 = ((f32[2,4,8,1024]{3,1,0,2:T(4,128)}), f32[2,4,8,1024]{3,1,0,2:T(4,128)S(1)}, u32[]{:S(2)}, u32[]{:S(2)}) async-start(f32[2,4,8,1024]{3,1,0,2:T(4,128)} %reshape.422), calls=%async_computation.2 | async-start | bytes 524288 | tf_op jit(solution)/shard_map/all_to_all | solution.py:50
  156.0 20.8 %all-to-all-start.7 = ((bf16[8,2,4096]{2,1,0:T(2,128)(2,1)}), bf16[8,2,4096]{2,1,0:T(2,128)(2,1)S(1)}, u32[]{:S(2)}, u32[]{:S(2)}) async-start(bf16[8,2,4096]{2,1,0:T(2,128)(2,1)} %reshape.435), calls=%async_computation.7 | async-start | bytes 262144 | tf_op jit(solution)/shard_map/all_to_all | solution.py:62
  162.4 19.4 %copy-start.13 = (s32[8,4]{0,1:T(4,128)S(1)}, s32[8,4]{0,1:T(4,128)}, u32[]{:S(2)}) copy-start(s32[8,4]{0,1:T(4,128)} %param.11) | copy-start | bytes 388
  176.7 26.5 %all-to-all-start.3 = ((bf16[8,2,4096]{2,1,0:T(2,128)(2,1)}), bf16[8,2,4096]{2,1,0:T(2,128)(2,1)S(1)}, u32[]{:S(2)}, u32[]{:S(2)}) async-start(bf16[8,2,4096]{2,1,0:T(2,128)(2,1)} %reshape.441), calls=%async_computation.3 | async-start | bytes 262144 | tf_op jit(solution)/shard_map/all_to_all | solution.py:62
  201.4 34.8 %collective-permute-start.4 = (bf16[1,8,1,4,256]{4,3,2,1,0:T(4,128)(2,1)S(1)}, bf16[1,8,1,4,256]{4,3,2,1,0:T(4,128)(2,1)S(1)}, u32[]{:S(2)}, u32[]{:S(2)}) collective-permute-start(bf16[1,8,1,4,256]{4,3,2,1,0:T(4,128)(2,1)S(1)} %get-tuple-element.30), channel_id=1, source_target_pairs={{0,8},{8,16},{16,24},{24,32},{32,40},{40,48},{48,56},{56,64},{64,7... | collective-permute-start | bytes 49160 | tf_op jit(solution)/shard_map/ppermute | solution.py:19
  229.6 6.7 collective-permute-start.5
  230.9 11.9 %collective-permute-start = (bf16[1,8,1,4,256]{4,3,2,1,0:T(4,128)(2,1)S(1)}, bf16[1,8,1,4,256]{4,3,2,1,0:T(4,128)(2,1)S(1)}, u32[]{:S(2)}, u32[]{:S(2)}) collective-permute-start(bf16[1,8,1,4,256]{4,3,2,1,0:T(4,128)(2,1)S(1)} %get-tuple-element.28), channel_id=1, source_target_pairs={{0,8},{8,16},{16,24},{24,32},{32,40},{40,48},{48,56},{56,64},{64,7... | collective-permute-start | bytes 49160 | tf_op jit(solution)/shard_map/ppermute | solution.py:19
  234.9 8.0 %collective-permute-start.1 = (bf16[1,8,1,4,256]{4,3,2,1,0:T(4,128)(2,1)S(1)}, bf16[1,8,1,4,256]{4,3,2,1,0:T(4,128)(2,1)S(1)}, u32[]{:S(2)}, u32[]{:S(2)}) collective-permute-start(bf16[1,8,1,4,256]{4,3,2,1,0:T(4,128)(2,1)S(1)} %get-tuple-element.27), channel_id=1, source_target_pairs={{8,0},{16,8},{24,16},{32,24},{40,32},{48,40},{56,48},{64,56},{72,6... | collective-permute-start | bytes 49160 | tf_op jit(solution)/shard_map/ppermute | solution.py:20
  236.5 12.8 %collective-permute-start.6 = (bf16[1,8,10,1,256]{4,3,2,1,0:T(2,128)(2,1)S(1)}, bf16[1,8,10,1,256]{4,3,2,1,0:T(2,128)(2,1)S(1)}, u32[]{:S(2)}, u32[]{:S(2)}) collective-permute-start(bf16[1,8,10,1,256]{4,3,2,1,0:T(2,128)(2,1)S(1)} %get-tuple-element.25), channel_id=1, source_target_pairs={{0,1},{1,2},{2,3},{3,4},{4,5},{5,6},{6,7},{8,9},{9,10},{10,11},{11... | collective-permute-start | bytes 122888 | tf_op jit(solution)/shard_map/ppermute | solution.py:19
  240.9 8.4 %collective-permute-start.7 = (bf16[1,8,10,1,256]{4,3,2,1,0:T(2,128)(2,1)S(1)}, bf16[1,8,10,1,256]{4,3,2,1,0:T(2,128)(2,1)S(1)}, u32[]{:S(2)}, u32[]{:S(2)}) collective-permute-start(bf16[1,8,10,1,256]{4,3,2,1,0:T(2,128)(2,1)S(1)} %get-tuple-element.26), channel_id=1, source_target_pairs={{1,0},{2,1},{3,2},{4,3},{5,4},{6,5},{7,6},{9,8},{10,9},{11,10},{12... | collective-permute-start | bytes 122888 | tf_op jit(solution)/shard_map/ppermute | solution.py:20
  243.7 17.3 %collective-permute-start.2 = (bf16[1,8,10,1,256]{4,3,2,1,0:T(2,128)(2,1)}, bf16[1,8,10,1,256]{4,3,2,1,0:T(2,128)(2,1)}, u32[]{:S(2)}, u32[]{:S(2)}) collective-permute-start(bf16[1,8,10,1,256]{4,3,2,1,0:T(2,128)(2,1)} %get-tuple-element.23), channel_id=1, source_target_pairs={{0,1},{1,2},{2,3},{3,4},{4,5},{5,6},{6,7},{8,9},{9,10},{10,11},{11... | collective-permute-start | bytes 122888 | tf_op jit(solution)/shard_map/ppermute | solution.py:19
  247.3 13.7 %collective-permute-start.3 = (bf16[1,8,10,1,256]{4,3,2,1,0:T(2,128)(2,1)}, bf16[1,8,10,1,256]{4,3,2,1,0:T(2,128)(2,1)}, u32[]{:S(2)}, u32[]{:S(2)}) collective-permute-start(bf16[1,8,10,1,256]{4,3,2,1,0:T(2,128)(2,1)} %get-tuple-element.24), channel_id=1, source_target_pairs={{1,0},{2,1},{3,2},{4,3},{5,4},{6,5},{7,6},{9,8},{10,9},{11,10},{12... | collective-permute-start | bytes 122888 | tf_op jit(solution)/shard_map/ppermute | solution.py:20
  261.0 8.0 %copy-start.15 = (pred[8,33]{0,1:T(8,128)(4,1)S(1)}, pred[8,33]{0,1:T(8,128)(4,1)}, u32[]{:S(2)}) copy-start(pred[8,33]{0,1:T(8,128)(4,1)} %constant.88) | copy-start | bytes 796
  262.2 6.8 copy-start.8
  269.0 9.1 %copy-start.2 = (bf16[8,10,6,1,8,33]{0,4,5,2,1,3:T(8,128)(2,1)S(1)}, bf16[8,10,6,1,8,33]{0,4,5,2,1,3:T(8,128)(2,1)}, u32[]{:S(2)}) copy-start(bf16[8,10,6,1,8,33]{0,4,5,2,1,3:T(8,128)(2,1)} %copy.347) | copy-start | bytes 760324
  269.0 9.1 %copy-start.14 = (bf16[8,16,3,3,3]{1,0,4,3,2:T(8,128)(2,1)S(1)}, bf16[8,16,3,3,3]{1,0,4,3,2:T(8,128)(2,1)}, u32[]{:S(2)}) copy-start(bf16[8,16,3,3,3]{1,0,4,3,2:T(8,128)(2,1)} %param.9) | copy-start | bytes 20740
  296.9 122.3 %collective-permute-start.12 = (bf16[1,16,1,4,256]{4,1,3,0,2:T(8,128)(2,1)}, bf16[1,16,1,4,256]{4,1,3,0,2:T(8,128)(2,1)}, u32[]{:S(2)}, u32[]{:S(2)}) collective-permute-start(bf16[1,16,1,4,256]{4,1,3,0,2:T(8,128)(2,1)} %slice_bitcast_fusion.4), channel_id=1, source_target_pairs={{0,8},{8,16},{16,24},{24,32},{32,40},{40,48},{48,56},{56,64},{64,7... | collective-permute-start | bytes 98312 | tf_op jit(solution)/shard_map/ppermute | solution.py:19
  303.2 116.0 %collective-permute-start.13 = (bf16[1,16,1,4,256]{4,1,3,0,2:T(8,128)(2,1)}, bf16[1,16,1,4,256]{4,1,3,0,2:T(8,128)(2,1)}, u32[]{:S(2)}, u32[]{:S(2)}) collective-permute-start(bf16[1,16,1,4,256]{4,1,3,0,2:T(8,128)(2,1)} %slice_bitcast_fusion.3), channel_id=1, source_target_pairs={{8,0},{16,8},{24,16},{32,24},{40,32},{48,40},{56,48},{64,56},{72,6... | collective-permute-start | bytes 98312 | tf_op jit(solution)/shard_map/ppermute | solution.py:20
  305.2 12.1 %copy-start.4 = (bf16[8,10,6,1,7,1]{5,4,2,1,0,3:T(8,128)(2,1)S(1)}, bf16[8,10,6,1,7,1]{5,4,2,1,0,3:T(8,128)(2,1)}, u32[]{:S(2)}) copy-start(bf16[8,10,6,1,7,1]{5,4,2,1,0,3:T(8,128)(2,1)} %get-tuple-element.12) | copy-start | bytes 20164
  306.7 13.5 %collective-permute-start.8 = (bf16[1,16,1,4,256]{4,1,3,0,2:T(8,128)(2,1)S(1)}, bf16[1,16,1,4,256]{4,1,3,0,2:T(8,128)(2,1)S(1)}, u32[]{:S(2)}, u32[]{:S(2)}) collective-permute-start(bf16[1,16,1,4,256]{4,1,3,0,2:T(8,128)(2,1)S(1)} %slice_bitcast_fusion.6), channel_id=1, source_target_pairs={{0,8},{8,16},{16,24},{24,32},{32,40},{40,48},{48,56},{56,64},{64,7... | collective-permute-start | bytes 98312 | tf_op jit(solution)/shard_map/ppermute | solution.py:19
  311.2 9.1 %collective-permute-start.9 = (bf16[1,16,1,4,256]{4,1,3,2,0:T(8,128)(2,1)S(1)}, bf16[1,16,1,4,256]{4,1,3,2,0:T(8,128)(2,1)S(1)}, u32[]{:S(2)}, u32[]{:S(2)}) collective-permute-start(bf16[1,16,1,4,256]{4,1,3,2,0:T(8,128)(2,1)S(1)} %slice_bitcast_fusion.5), channel_id=1, source_target_pairs={{8,0},{16,8},{24,16},{32,24},{40,32},{48,40},{56,48},{64,56},{72,6... | collective-permute-start | bytes 98312 | tf_op jit(solution)/shard_map/ppermute | solution.py:20
  320.3 16.8 %collective-permute-start.10 = (bf16[1,16,10,1,256]{4,1,3,2,0:T(8,128)(2,1)S(1)}, bf16[1,16,10,1,256]{4,1,3,2,0:T(8,128)(2,1)S(1)}, u32[]{:S(2)}, u32[]{:S(2)}) collective-permute-start(bf16[1,16,10,1,256]{4,1,3,2,0:T(8,128)(2,1)S(1)} %get-tuple-element.17), channel_id=1, source_target_pairs={{0,1},{1,2},{2,3},{3,4},{4,5},{5,6},{6,7},{8,9},{9,10},{10,11},{11... | collective-permute-start | bytes 245768 | tf_op jit(solution)/shard_map/ppermute | solution.py:19
  324.8 12.3 %collective-permute-start.11 = (bf16[1,16,10,1,256]{4,1,3,2,0:T(8,128)(2,1)S(1)}, bf16[1,16,10,1,256]{4,1,3,2,0:T(8,128)(2,1)}, u32[]{:S(2)}, u32[]{:S(2)}) collective-permute-start(bf16[1,16,10,1,256]{4,1,3,2,0:T(8,128)(2,1)S(1)} %get-tuple-element.18), channel_id=1, source_target_pairs={{1,0},{2,1},{3,2},{4,3},{5,4},{6,5},{7,6},{9,8},{10,9},{11,10},{12... | collective-permute-start | bytes 245768 | tf_op jit(solution)/shard_map/ppermute | solution.py:20
  330.7 3.5 copy-start.3
  368.4 58.1 %all-to-all-start.8 = ((f32[32,1,2048]{2,1,0:T(1,128)}), f32[32,1,2048]{2,1,0:T(1,128)S(1)}, u32[]{:S(2)}, u32[]{:S(2)}) async-start(f32[32,1,2048]{2,1,0:T(1,128)} %reshape.443), calls=%async_computation.8 | async-start | bytes 524288 | tf_op jit(solution)/shard_map/all_to_all | solution.py:47
  420.6 61.2 %collective-permute-start.14 = (bf16[1,16,10,1,256]{4,1,3,2,0:T(8,128)(2,1)}, bf16[1,16,10,1,256]{4,1,3,2,0:T(8,128)(2,1)}, u32[]{:S(2)}, u32[]{:S(2)}) collective-permute-start(bf16[1,16,10,1,256]{4,1,3,2,0:T(8,128)(2,1)} %get-tuple-element.13), channel_id=1, source_target_pairs={{0,1},{1,2},{2,3},{3,4},{4,5},{5,6},{6,7},{8,9},{9,10},{10,11},{11... | collective-permute-start | bytes 245768 | tf_op jit(solution)/shard_map/ppermute | solution.py:19
  424.5 57.3 %collective-permute-start.15 = (bf16[1,16,10,1,256]{4,1,3,2,0:T(8,128)(2,1)}, bf16[1,16,10,1,256]{4,1,3,2,0:T(8,128)(2,1)}, u32[]{:S(2)}, u32[]{:S(2)}) collective-permute-start(bf16[1,16,10,1,256]{4,1,3,2,0:T(8,128)(2,1)} %get-tuple-element.14), channel_id=1, source_target_pairs={{1,0},{2,1},{3,2},{4,3},{5,4},{6,5},{7,6},{9,8},{10,9},{11,10},{12... | collective-permute-start | bytes 245768 | tf_op jit(solution)/shard_map/ppermute | solution.py:20
  434.2 24.7 %copy-start.5 = (bf16[8,4,8,33,16]{4,2,3,1,0:T(8,128)(2,1)S(1)}, bf16[8,4,8,33,16]{4,2,3,1,0:T(8,128)(2,1)}, u32[]{:S(2)}) copy-start(bf16[8,4,8,33,16]{4,2,3,1,0:T(8,128)(2,1)} %multiply_convert_fusion) | copy-start | bytes 811012
  446.6 48.2 %all-to-all-start.9 = ((f32[32,1,2048]{2,1,0:T(1,128)}), f32[32,1,2048]{2,1,0:T(1,128)S(1)}, u32[]{:S(2)}, u32[]{:S(2)}) async-start(f32[32,1,2048]{2,1,0:T(1,128)} %reshape.445), calls=%async_computation.9 | async-start | bytes 524288 | tf_op jit(solution)/shard_map/all_to_all | solution.py:51
  498.6 178.5 %all-to-all-start.10 = ((f32[2,4,8,1024]{3,1,0,2:T(4,128)}), f32[2,4,8,1024]{3,1,0,2:T(4,128)S(1)}, u32[]{:S(2)}, u32[]{:S(2)}) async-start(f32[2,4,8,1024]{3,1,0,2:T(4,128)} %reshape.426), calls=%async_computation.10 | async-start | bytes 524288 | tf_op jit(solution)/shard_map/all_to_all | solution.py:50
  504.1 90.1 %copy-start.11 = (f32[16,8,3,3,3]{0,1,4,3,2:T(8,128)S(1)}, f32[16,8,3,3,3]{0,1,4,3,2:T(8,128)}, u32[]{:S(2)}) copy-start(f32[16,8,3,3,3]{0,1,4,3,2:T(8,128)} %fusion.52) | copy-start | bytes 41476
  504.1 173.3 %copy-start.9 = (f32[1,2,32,32]{3,2,1,0:T(8,128)S(1)}, f32[1,2,32,32]{3,2,1,0:T(8,128)}, u32[]{:S(2)}) copy-start(f32[1,2,32,32]{3,2,1,0:T(8,128)} %get-tuple-element.31) | copy-start | bytes 24580
  504.1 173.3 %copy-start.10 = (f32[1,2,32,32]{3,2,1,0:T(8,128)S(1)}, f32[1,2,32,32]{3,2,1,0:T(8,128)}, u32[]{:S(2)}) copy-start(f32[1,2,32,32]{3,2,1,0:T(8,128)} %get-tuple-element.32) | copy-start | bytes 24580
  692.1 9.8 %all-to-all-start.11 = ((bf16[8,2,4096]{2,1,0:T(2,128)(2,1)}), bf16[8,2,4096]{2,1,0:T(2,128)(2,1)S(1)}, u32[]{:S(2)}, u32[]{:S(2)}) async-start(bf16[8,2,4096]{2,1,0:T(2,128)(2,1)} %reshape.447), calls=%async_computation.11 | async-start | bytes 262144 | tf_op jit(solution)/shard_map/all_to_all | solution.py:62
  696.1 26.4 %copy-start.1 = (bf16[16,8,3,3,3]{0,1,4,3,2:T(8,128)(2,1)S(1)}, bf16[16,8,3,3,3]{0,1,4,3,2:T(8,128)(2,1)}, u32[]{:S(2)}) copy-start(bf16[16,8,3,3,3]{0,1,4,3,2:T(8,128)(2,1)} %param.8) | copy-start | bytes 20740
  696.8 24.9 %copy-start.7 = (f32[2,4,8,4,256]{4,3,2,1,0:T(4,128)S(1)}, f32[2,4,8,4,256]{4,3,2,1,0:T(4,128)}, u32[]{:S(2)}) copy-start(f32[2,4,8,4,256]{4,3,2,1,0:T(4,128)} %param.7) | copy-start | bytes 786436
  696.8 24.9 %copy-start.12 = (f32[8,4]{1,0:T(8,128)S(1)}, f32[8,4]{1,0:T(8,128)}, u32[]{:S(2)}) copy-start(f32[8,4]{1,0:T(8,128)} %copy.333) | copy-start | bytes 388
where the time goes:
time: 732 us; the launch traced here: 723 us
  local copies, waits for them, and re-layouts  264 us (36%)
  starting transfers between devices  175 us (24%)
  matrix products  151 us (21%)
  blocking collectives  82.3 us (11%)
  other arithmetic  28 us (4%)
  waiting for transfers between devices  19.7 us (3%)
    unnamed x60, local copies, waits for them, and re-layouts  126 us
    transpose x2, matrix products, kernel_gradient(): return summed.transpose(1, 0, 2, 3, 4)  113 us
    psum x1, blocking collectives, local(): summed_in, summed_out = lax.psum((local_in, local_out), ('gy', 'gz'))  82.3 us
    all_to_all x3, starting transfers between devices, spectral(): lax.all_to_all(flattened, 'gy', split_axis=3, concat_axis=2, tiled=True)  62.5 us
    all_to_all x3, starting transfers between devices, spectral(): lax.all_to_all(transformed_y, 'gy', split_axis=2, concat_axis=3, tiled=True)  36.1 us
    ppermute x8, starting transfers between devices, extended(): before = lax.ppermute(last, axis, up)  31.5 us
    conv_general_dilated x3, matrix products, convolve(): lax.conv_general_dilated(padded, kernel, (1, 1, 1), ((0, 0), (0, 0), (1,...  27.8 us
    conv_general_dilated x12, local copies, waits for them, and re-layouts, convolve(): lax.conv_general_dilated(padded, kernel, (1, 1, 1), ((0, 0), (0, 0), (1,...  25.1 us
  transfers between devices with their start and end apart: 28, of which 4 were waited for; matrix products, arithmetic and copies ran while one was open for 49% of the time, Pallas kernels for 0%

commit v1 on v0

--- a/solution.py
+++ b/solution.py
@@ -3,6 +3,11 @@
 import jax.numpy as jnp
 from jax import lax
 from jax.sharding import PartitionSpec as P
+
+
+def by_each_axis(value, leading, second):
+    inner = lax.psum(value, leading)
+    return lax.psum(inner, second)
 
 
 def as_sent(shard):
@@ -120,7 +125,7 @@
     hidden_padded = with_rims(back_hidden)
     back_image = convolve(hidden_padded, flipped(weight_in))
     spectrum = spectral(back_image.reshape(2, coil_count, cells_y, cells_z, readout), -1.0)
-    summed_in, summed_out = lax.psum((local_in, local_out), ("gy", "gz"))
+    summed_in, summed_out = by_each_axis((local_in, local_out), "gy", "gz")
     scale = 1.0 / math.sqrt(voxels)
     mask_field = sampling_mask.astype(jnp.float32)[None, None, :, :, None]
     grad_kspace = cotangent - consistency_weight[0] * mask_field * cotangent + spectrum

time: 732 us -> 903 us (1.23)
  blocking collectives: 82.3 us -> 251 us
    psum x1 -> x2, blocking collectives: 82.3 us -> 251 us  [the longest x1 199 us: by_each_axis(): inner = lax.psum(value, leading)]
  transfers between devices with their start and end apart: 28 -> 28, of which waited for: 4 -> 4; matrix products, arithmetic and copies ran while one was open for 49% -> 40% of each run, Pallas kernels for 0% -> 0%
where the time goes in v1:
time: 903 us; the launch traced here: 895 us
  local copies, waits for them, and re-layouts  264 us (29%)
  blocking collectives  251 us (28%)
  starting transfers between devices  178 us (20%)
  matrix products  152 us (17%)
  other arithmetic  27.7 us (3%)
  waiting for transfers between devices  19.8 us (2%)
    psum x1, blocking collectives, by_each_axis(): inner = lax.psum(value, leading)  199 us
    unnamed x60, local copies, waits for them, and re-layouts  126 us
    transpose x2, matrix products, kernel_gradient(): return summed.transpose(1, 0, 2, 3, 4)  113 us
    all_to_all x3, starting transfers between devices, spectral(): lax.all_to_all(flattened, 'gy', split_axis=3, concat_axis=2, tiled=True)  62.5 us
    psum x1, blocking collectives, by_each_axis(): return lax.psum(inner, second)  52.4 us
    all_to_all x3, starting transfers between devices, spectral(): lax.all_to_all(transformed_y, 'gy', split_axis=2, concat_axis=3, tiled=True)  36.1 us
    ppermute x8, starting transfers between devices, extended(): before = lax.ppermute(last, axis, up)  31.5 us
    conv_general_dilated x3, matrix products, convolve(): lax.conv_general_dilated(padded, kernel, (1, 1, 1), ((0, 0), (0, 0), (1,...  27.8 us
  transfers between devices with their start and end apart: 28, of which 4 were waited for; matrix products, arithmetic and copies ran while one was open for 40% of the time, Pallas kernels for 0%

profile of v1, /device:TPU:1, one launch (start us, length us, event | category | flops | bytes accessed | tf_op | source)
XLA Modules:
  0.0 894.5 jit_solution(17645300207764178170)
XLA Ops:
  0.7 4.5 copy.348
  5.1 6.9 reshape.431
  12.0 14.5 %all-to-all-start.4 = ((f32[32,1,2048]{2,1,0:T(1,128)}), f32[32,1,2048]{2,1,0:T(1,128)S(1)}, u32[]{:S(2)}, u32[]{:S(2)}) async-start(f32[32,1,2048]{2,1,0:T(1,128)} %reshape.431), calls=%async_computation.4 | async-start | bytes 524288 | tf_op jit(solution)/shard_map/all_to_all | solution.py:52
  29.7 6.9 reshape.437
  38.5 11.0 %all-to-all-start = ((f32[32,1,2048]{2,1,0:T(1,128)}), f32[32,1,2048]{2,1,0:T(1,128)S(1)}, u32[]{:S(2)}, u32[]{:S(2)}) async-start(f32[32,1,2048]{2,1,0:T(1,128)} %reshape.437), calls=%async_computation | async-start | bytes 524288 | tf_op jit(solution)/shard_map/all_to_all | solution.py:52
  54.5 6.3 reshape.432
  60.9 3.5 copy.417
  68.3 12.0 %all-to-all-start.5 = ((f32[32,1,2048]{2,1,0:T(1,128)}), f32[32,1,2048]{2,1,0:T(1,128)S(1)}, u32[]{:S(2)}, u32[]{:S(2)}) async-start(f32[32,1,2048]{2,1,0:T(1,128)} %reshape.433), calls=%async_computation.5 | async-start | bytes 524288 | tf_op jit(solution)/shard_map/all_to_all | solution.py:56
  81.5 6.3 reshape.438
  87.9 3.5 copy.411
  95.3 11.8 %all-to-all-start.1 = ((f32[32,1,2048]{2,1,0:T(1,128)}), f32[32,1,2048]{2,1,0:T(1,128)S(1)}, u32[]{:S(2)}, u32[]{:S(2)}) async-start(f32[32,1,2048]{2,1,0:T(1,128)} %reshape.439), calls=%async_computation.1 | async-start | bytes 524288 | tf_op jit(solution)/shard_map/all_to_all | solution.py:56
  110.5 8.6 all-to-all-done.1
  119.1 7.4 all-to-all-start.6
  130.1 5.2 all-to-all-done.6
  135.2 4.8 all-to-all-start.2
  141.5 4.9 copy.421
  146.4 9.3 %reshape.435 = bf16[8,2,4096]{2,1,0:T(2,128)(2,1)} reshape(bf16[8192,1,2,4]{3,2,1,0:T(2,128)(2,1)} %bitcast.299) | data formatting | bytes 262144
  155.8 5.1 all-to-all-start.7
  162.2 4.9 copy.415
  167.1 9.3 %reshape.441 = bf16[8,2,4096]{2,1,0:T(2,128)(2,1)} reshape(bf16[8192,1,2,4]{3,2,1,0:T(2,128)(2,1)} %bitcast.300) | data formatting | bytes 262144
  176.5 5.1 all-to-all-start.3
  182.3 10.0 %reshape.436 = bf16[8192,1,2,4]{3,2,1,0:T(2,128)(2,1)} reshape(bf16[8,2,4096]{2,1,0:T(2,128)(2,1)S(1)} %all-to-all-done.7) | data formatting | bytes 262144
  192.3 8.6 copy.358
  203.0 10.0 %reshape.442 = bf16[8192,1,2,4]{3,2,1,0:T(2,128)(2,1)} reshape(bf16[8,2,4096]{2,1,0:T(2,128)(2,1)S(1)} %all-to-all-done.3) | data formatting | bytes 262144
  213.0 8.6 copy.344
  221.9 7.4 copy.396
  230.6 4.0 collective-permute-start
  236.1 4.4 collective-permute-start.6
  243.3 3.6 collective-permute-start.2
  254.2 4.8 copy.361
  262.9 4.6 copy.347
  268.7 9.1 %multiply_convert_fusion.1 = (bf16[8,4,8,33,16]{4,2,3,1,0:T(8,128)(2,1)}, f32[8,4,8,33,16]{4,2,3,1,0:T(8,128)S(1)}) fusion(pred[8,33]{0,1:T(8,128)(4,1)S(1)} %copy-done.15, bf16[16,8,3,3,3]{0,1,4,3,2:T(8,128)(2,1)S(1)} %copy-done, bf16[8,10,6,1,7,2]{0,4,5,2,1,3:T(8,128)(2,1)S(1)} %copy-done.8, bf16[8,10,6,1,8,33]{0,4,5,2,1,3:T(8,128)(2,1)} %copy.361), kind=kOutput, calls=%fused_computation.16 | convolution fusion | flops 60009984 | bytes 1085064 | tf_op jit(solution)/shard_map/conv_general_dilated | solution.py:78
  277.8 9.5 %multiply_convert_fusion = bf16[8,4,8,33,16]{4,2,3,1,0:T(8,128)(2,1)} fusion(f32[8,4,8,33,16]{4,2,3,1,0:T(8,128)S(1)} %get-tuple-element.38, bf16[8,16,3,3,3]{1,0,4,3,2:T(8,128)(2,1)S(1)} %copy-done.14, bf16[8,10,6,1,7,2]{0,4,5,2,1,3:T(8,128)(2,1)S(1)} %slice.86, bf16[8,10,6,1,8,33]{0,4,5,2,1,3:T(8,128)(2,1)S(1)} %copy-done.2, pred[8,33]{0,1:T(8,128)(4,1)S(1)} %copy-done.15), kind=kOutput, calls=%fused_computation.15 | convolution fusion | flops 60685824 | bytes 1085064 | tf_op jit(solution)/shard_map/conv_general_dilated | solution.py:78
  287.3 3.7 copy.363
  296.5 5.3 collective-permute-start.12
  306.4 4.0 collective-permute-start.8
  312.1 4.8 copy.442
  319.9 4.5 collective-permute-start.10
  326.3 4.0 fusion.33
  330.3 3.5 copy.441
  339.8 4.8 copy.368
  345.6 9.1 %broadcast_select_fusion = f32[8,4,8,33,8]{4,2,3,1,0:T(8,128)} fusion(pred[8,33]{0,1:T(8,128)(4,1)S(1)} %copy-done.15, bf16[16,8,3,3,3]{0,1,4,3,2:T(8,128)(2,1)S(1)} %copy-done, bf16[16,10,6,1,7,2]{0,4,5,2,1,3:T(8,128)(2,1)S(1)} %slice.97, bf16[16,10,6,1,8,33]{0,4,5,2,1,3:T(8,128)(2,1)} %copy.368), kind=kOutput, calls=%fused_computation.41 | convolution fusion | flops 60072960 | bytes 811272 | tf_op jit(solution)/shard_map/conv_general_dilated | solution.py:78
  361.2 6.9 reshape.443
  368.1 37.0 %all-to-all-start.8 = ((f32[32,1,2048]{2,1,0:T(1,128)}), f32[32,1,2048]{2,1,0:T(1,128)S(1)}, u32[]{:S(2)}, u32[]{:S(2)}) async-start(f32[32,1,2048]{2,1,0:T(1,128)} %reshape.443), calls=%async_computation.8 | async-start | bytes 524288 | tf_op jit(solution)/shard_map/all_to_all | solution.py:52
  405.1 3.9 fusion.35
  409.0 3.7 copy.391
  414.4 4.5 copy.388
  420.4 3.9 collective-permute-start.14
  427.5 6.4 reshape.444
  433.9 3.7 copy.436
  437.5 5.4 convolution_bitcast_fusion.5
  446.3 12.3 %all-to-all-start.9 = ((f32[32,1,2048]{2,1,0:T(1,128)}), f32[32,1,2048]{2,1,0:T(1,128)S(1)}, u32[]{:S(2)}, u32[]{:S(2)}) async-start(f32[32,1,2048]{2,1,0:T(1,128)} %reshape.445), calls=%async_computation.9 | async-start | bytes 524288 | tf_op jit(solution)/shard_map/all_to_all | solution.py:56
  458.6 22.9 %fusion.52 = f32[16,8,3,3,3]{0,1,4,3,2:T(8,128)} fusion(bf16[8,4,8,33,16]{4,2,3,1,0:T(8,128)(2,1)S(1)} %copy-done.5, pred[8,33]{0,1:T(8,128)(4,1)S(1)} %copy-done.15, bf16[8,10,6,8,33,1]{3,0,5,4,2,1:T(8,128)(2,1)} %fusion.33, bf16[8,10,6,8,33,1]{3,0,5,4,2,1:T(8,128)(2,1)} %copy.388, bf16[8,10,6,8,33,1]{3,0,5,4,2,1:T(8,128)(2,1)} %fusion.35), kind=kOutput, calls=%fused_computation.59 | convolution fusion | flops 59288064 | bytes 1044744 | tf_op jit(solution)/shard_map/transpose | solution.py:97
  482.5 11.9 %copy.395 = bf16[1,16,10,6,256]{1,0,4,3,2:T(2,128)(2,1)} copy(bf16[1,16,10,6,256]{4,1,3,2,0:T(8,128)(2,1)S(1)} %pad_maximum_fusion.7) | data formatting | bytes 983040 | tf_op jit(solution)/shard_map/concatenate | solution.py:26
  498.2 5.5 all-to-all-start.10
  503.7 90.1 %fusion.123 = f32[8,16,3,3,3]{1,0,4,3,2:T(8,128)S(1)} fusion(bf16[1,16,10,6,256]{1,0,4,3,2:T(2,128)(2,1)} %copy.395, bf16[1,8,8,4,256]{1,0,4,3,2:T(2,128)(2,1)} %copy.396), kind=kOutput, calls=%fused_computation.182 | convolution fusion | flops 56475648 | bytes 636416 | tf_op jit(solution)/shard_map/transpose | solution.py:97
  593.8 198.7 %all-reduce = (f32[16,8,3,3,3]{0,1,4,3,2:T(8,128)S(1)}, f32[8,16,3,3,3]{1,0,4,3,2:T(8,128)S(1)}) all-reduce(f32[16,8,3,3,3]{0,1,4,3,2:T(8,128)S(1)} %copy-done.11, f32[8,16,3,3,3]{1,0,4,3,2:T(8,128)S(1)} %fusion.123), channel_id=1, replica_groups=mesh['gy'=32,'gz'=8] {'gy'}, use_global_device_ids=true, to_apply=%region_0.1 | all-reduce | flops 6912 | bytes 55296 | tf_op jit(solution)/shard_map/psum | solution.py:9
  792.5 52.4 %all-reduce.1 = (f32[16,8,3,3,3]{0,1,4,3,2:T(8,128)S(1)}, f32[8,16,3,3,3]{1,0,4,3,2:T(8,128)S(1)}) all-reduce(f32[16,8,3,3,3]{0,1,4,3,2:T(8,128)S(1)} %get-tuple-element.3, f32[8,16,3,3,3]{1,0,4,3,2:T(8,128)S(1)} %get-tuple-element.4), channel_id=1, replica_groups=mesh['gy'=32,'gz'=8] {'gz'}, use_global_device_ids=true, to_apply=%region_1.2 | all-reduce | flops 6912 | bytes 55296 | tf_op jit(solution)/shard_map/psum | solution.py:10
  846.2 5.0 copy.428
  851.2 9.3 %reshape.447 = bf16[8,2,4096]{2,1,0:T(2,128)(2,1)} reshape(bf16[8192,1,2,4]{3,2,1,0:T(2,128)(2,1)} %bitcast.304) | data formatting | bytes 262144
  860.5 7.4 all-to-all-start.11
  868.6 5.2 all-to-all-done.11
  873.8 10.0 %reshape.448 = bf16[8192,1,2,4]{3,2,1,0:T(2,128)(2,1)} reshape(bf16[8,2,4096]{2,1,0:T(2,128)(2,1)S(1)} %all-to-all-done.11) | data formatting | bytes 262144
  883.8 9.6 %copy.381 = f32[2,4,8,4,256]{4,3,2,1,0:T(4,128)S(1)} copy(bf16[2,4,8,4,256]{1,0,4,3,2:T(2,128)(2,1)} %bitcast.305) | data formatting | bytes 393216 | tf_op jit(solution)/shard_map/convert_element_type | solution.py:69
  (173 shorter events, 96.1 us)
Async XLA Ops:
  0.6 268.0 %copy-start = (bf16[16,8,3,3,3]{0,1,4,3,2:T(8,128)(2,1)S(1)}, bf16[16,8,3,3,3]{0,1,4,3,2:T(8,128)(2,1)}, u32[]{:S(2)}) copy-start(bf16[16,8,3,3,3]{0,1,4,3,2:T(8,128)(2,1)} %param.8) | copy-start | bytes 20740
  0.6 25.9 %copy-start.6 = (f32[2,4,8,4,256]{4,3,2,1,0:T(4,128)S(1)}, f32[2,4,8,4,256]{4,3,2,1,0:T(4,128)}, u32[]{:S(2)}) copy-start(f32[2,4,8,4,256]{4,3,2,1,0:T(4,128)} %param.7) | copy-start | bytes 786436
  12.0 26.5 %all-to-all-start.4 = ((f32[32,1,2048]{2,1,0:T(1,128)}), f32[32,1,2048]{2,1,0:T(1,128)S(1)}, u32[]{:S(2)}, u32[]{:S(2)}) async-start(f32[32,1,2048]{2,1,0:T(1,128)} %reshape.431), calls=%async_computation.4 | async-start | bytes 524288 | tf_op jit(solution)/shard_map/all_to_all | solution.py:52
  38.5 29.8 %all-to-all-start = ((f32[32,1,2048]{2,1,0:T(1,128)}), f32[32,1,2048]{2,1,0:T(1,128)S(1)}, u32[]{:S(2)}, u32[]{:S(2)}) async-start(f32[32,1,2048]{2,1,0:T(1,128)} %reshape.437), calls=%async_computation | async-start | bytes 524288 | tf_op jit(solution)/shard_map/all_to_all | solution.py:52
  68.3 27.0 %all-to-all-start.5 = ((f32[32,1,2048]{2,1,0:T(1,128)}), f32[32,1,2048]{2,1,0:T(1,128)S(1)}, u32[]{:S(2)}, u32[]{:S(2)}) async-start(f32[32,1,2048]{2,1,0:T(1,128)} %reshape.433), calls=%async_computation.5 | async-start | bytes 524288 | tf_op jit(solution)/shard_map/all_to_all | solution.py:56
  95.3 23.8 %all-to-all-start.1 = ((f32[32,1,2048]{2,1,0:T(1,128)}), f32[32,1,2048]{2,1,0:T(1,128)S(1)}, u32[]{:S(2)}, u32[]{:S(2)}) async-start(f32[32,1,2048]{2,1,0:T(1,128)} %reshape.439), calls=%async_computation.1 | async-start | bytes 524288 | tf_op jit(solution)/shard_map/all_to_all | solution.py:56
  119.1 16.2 %all-to-all-start.6 = ((f32[2,4,8,1024]{3,1,0,2:T(4,128)}), f32[2,4,8,1024]{3,1,0,2:T(4,128)S(1)}, u32[]{:S(2)}, u32[]{:S(2)}) async-start(f32[2,4,8,1024]{3,1,0,2:T(4,128)} %reshape.424), calls=%async_computation.6 | async-start | bytes 524288 | tf_op jit(solution)/shard_map/all_to_all | solution.py:55
  135.2 20.5 %all-to-all-start.2 = ((f32[2,4,8,1024]{3,1,0,2:T(4,128)}), f32[2,4,8,1024]{3,1,0,2:T(4,128)S(1)}, u32[]{:S(2)}, u32[]{:S(2)}) async-start(f32[2,4,8,1024]{3,1,0,2:T(4,128)} %reshape.422), calls=%async_computation.2 | async-start | bytes 524288 | tf_op jit(solution)/shard_map/all_to_all | solution.py:55
  155.8 20.7 %all-to-all-start.7 = ((bf16[8,2,4096]{2,1,0:T(2,128)(2,1)}), bf16[8,2,4096]{2,1,0:T(2,128)(2,1)S(1)}, u32[]{:S(2)}, u32[]{:S(2)}) async-start(bf16[8,2,4096]{2,1,0:T(2,128)(2,1)} %reshape.435), calls=%async_computation.7 | async-start | bytes 262144 | tf_op jit(solution)/shard_map/all_to_all | solution.py:67
  162.2 19.4 %copy-start.13 = (s32[8,4]{0,1:T(4,128)S(1)}, s32[8,4]{0,1:T(4,128)}, u32[]{:S(2)}) copy-start(s32[8,4]{0,1:T(4,128)} %param.11) | copy-start | bytes 388
  176.5 26.5 %all-to-all-start.3 = ((bf16[8,2,4096]{2,1,0:T(2,128)(2,1)}), bf16[8,2,4096]{2,1,0:T(2,128)(2,1)S(1)}, u32[]{:S(2)}, u32[]{:S(2)}) async-start(bf16[8,2,4096]{2,1,0:T(2,128)(2,1)} %reshape.441), calls=%async_computation.3 | async-start | bytes 262144 | tf_op jit(solution)/shard_map/all_to_all | solution.py:67
  201.1 34.8 %collective-permute-start.4 = (bf16[1,8,1,4,256]{4,3,2,1,0:T(4,128)(2,1)S(1)}, bf16[1,8,1,4,256]{4,3,2,1,0:T(4,128)(2,1)S(1)}, u32[]{:S(2)}, u32[]{:S(2)}) collective-permute-start(bf16[1,8,1,4,256]{4,3,2,1,0:T(4,128)(2,1)S(1)} %get-tuple-element.32), channel_id=1, source_target_pairs={{0,8},{8,16},{16,24},{24,32},{32,40},{40,48},{48,56},{56,64},{64,7... | collective-permute-start | bytes 49160 | tf_op jit(solution)/shard_map/ppermute | solution.py:24
  229.3 6.7 collective-permute-start.5
  230.6 11.9 %collective-permute-start = (bf16[1,8,1,4,256]{4,3,2,1,0:T(4,128)(2,1)S(1)}, bf16[1,8,1,4,256]{4,3,2,1,0:T(4,128)(2,1)S(1)}, u32[]{:S(2)}, u32[]{:S(2)}) collective-permute-start(bf16[1,8,1,4,256]{4,3,2,1,0:T(4,128)(2,1)S(1)} %get-tuple-element.30), channel_id=1, source_target_pairs={{0,8},{8,16},{16,24},{24,32},{32,40},{40,48},{48,56},{56,64},{64,7... | collective-permute-start | bytes 49160 | tf_op jit(solution)/shard_map/ppermute | solution.py:24
  234.5 8.0 collective-permute-start.1
  236.1 12.8 %collective-permute-start.6 = (bf16[1,8,10,1,256]{4,3,2,1,0:T(2,128)(2,1)S(1)}, bf16[1,8,10,1,256]{4,3,2,1,0:T(2,128)(2,1)S(1)}, u32[]{:S(2)}, u32[]{:S(2)}) collective-permute-start(bf16[1,8,10,1,256]{4,3,2,1,0:T(2,128)(2,1)S(1)} %get-tuple-element.27), channel_id=1, source_target_pairs={{0,1},{1,2},{2,3},{3,4},{4,5},{5,6},{6,7},{8,9},{9,10},{10,11},{11... | collective-permute-start | bytes 122888 | tf_op jit(solution)/shard_map/ppermute | solution.py:24
  240.5 8.4 collective-permute-start.7
  243.3 17.3 %collective-permute-start.2 = (bf16[1,8,10,1,256]{4,3,2,1,0:T(2,128)(2,1)}, bf16[1,8,10,1,256]{4,3,2,1,0:T(2,128)(2,1)}, u32[]{:S(2)}, u32[]{:S(2)}) collective-permute-start(bf16[1,8,10,1,256]{4,3,2,1,0:T(2,128)(2,1)} %get-tuple-element.25), channel_id=1, source_target_pairs={{0,1},{1,2},{2,3},{3,4},{4,5},{5,6},{6,7},{8,9},{9,10},{10,11},{11... | collective-permute-start | bytes 122888 | tf_op jit(solution)/shard_map/ppermute | solution.py:24
  247.0 13.7 %collective-permute-start.3 = (bf16[1,8,10,1,256]{4,3,2,1,0:T(2,128)(2,1)}, bf16[1,8,10,1,256]{4,3,2,1,0:T(2,128)(2,1)}, u32[]{:S(2)}, u32[]{:S(2)}) collective-permute-start(bf16[1,8,10,1,256]{4,3,2,1,0:T(2,128)(2,1)} %get-tuple-element.26), channel_id=1, source_target_pairs={{1,0},{2,1},{3,2},{4,3},{5,4},{6,5},{7,6},{9,8},{10,9},{11,10},{12... | collective-permute-start | bytes 122888 | tf_op jit(solution)/shard_map/ppermute | solution.py:25
  260.6 8.0 copy-start.15
  261.9 6.8 copy-start.8
  268.6 9.1 %copy-start.2 = (bf16[8,10,6,1,8,33]{0,4,5,2,1,3:T(8,128)(2,1)S(1)}, bf16[8,10,6,1,8,33]{0,4,5,2,1,3:T(8,128)(2,1)}, u32[]{:S(2)}) copy-start(bf16[8,10,6,1,8,33]{0,4,5,2,1,3:T(8,128)(2,1)} %copy.347) | copy-start | bytes 760324
  268.6 9.1 %copy-start.14 = (bf16[8,16,3,3,3]{1,0,4,3,2:T(8,128)(2,1)S(1)}, bf16[8,16,3,3,3]{1,0,4,3,2:T(8,128)(2,1)}, u32[]{:S(2)}) copy-start(bf16[8,16,3,3,3]{1,0,4,3,2:T(8,128)(2,1)} %param.9) | copy-start | bytes 20740
  296.5 122.4 %collective-permute-start.12 = (bf16[1,16,1,4,256]{4,1,3,0,2:T(8,128)(2,1)}, bf16[1,16,1,4,256]{4,1,3,0,2:T(8,128)(2,1)}, u32[]{:S(2)}, u32[]{:S(2)}) collective-permute-start(bf16[1,16,1,4,256]{4,1,3,0,2:T(8,128)(2,1)} %slice_bitcast_fusion.4), channel_id=1, source_target_pairs={{0,8},{8,16},{16,24},{24,32},{32,40},{40,48},{48,56},{56,64},{64,7... | collective-permute-start | bytes 98312 | tf_op jit(solution)/shard_map/ppermute | solution.py:24
  302.9 116.1 %collective-permute-start.13 = (bf16[1,16,1,4,256]{4,1,3,0,2:T(8,128)(2,1)}, bf16[1,16,1,4,256]{4,1,3,0,2:T(8,128)(2,1)}, u32[]{:S(2)}, u32[]{:S(2)}) collective-permute-start(bf16[1,16,1,4,256]{4,1,3,0,2:T(8,128)(2,1)} %slice_bitcast_fusion.3), channel_id=1, source_target_pairs={{8,0},{16,8},{24,16},{32,24},{40,32},{48,40},{56,48},{64,56},{72,6... | collective-permute-start | bytes 98312 | tf_op jit(solution)/shard_map/ppermute | solution.py:25
  304.9 12.1 %copy-start.4 = (bf16[8,10,6,1,7,1]{5,4,2,1,0,3:T(8,128)(2,1)S(1)}, bf16[8,10,6,1,7,1]{5,4,2,1,0,3:T(8,128)(2,1)}, u32[]{:S(2)}) copy-start(bf16[8,10,6,1,7,1]{5,4,2,1,0,3:T(8,128)(2,1)} %get-tuple-element.14) | copy-start | bytes 20164
  306.4 13.5 %collective-permute-start.8 = (bf16[1,16,1,4,256]{4,1,3,0,2:T(8,128)(2,1)S(1)}, bf16[1,16,1,4,256]{4,1,3,0,2:T(8,128)(2,1)S(1)}, u32[]{:S(2)}, u32[]{:S(2)}) collective-permute-start(bf16[1,16,1,4,256]{4,1,3,0,2:T(8,128)(2,1)S(1)} %slice_bitcast_fusion.6), channel_id=1, source_target_pairs={{0,8},{8,16},{16,24},{24,32},{32,40},{40,48},{48,56},{56,64},{64,7... | collective-permute-start | bytes 98312 | tf_op jit(solution)/shard_map/ppermute | solution.py:24
  310.8 9.1 %collective-permute-start.9 = (bf16[1,16,1,4,256]{4,1,3,2,0:T(8,128)(2,1)S(1)}, bf16[1,16,1,4,256]{4,1,3,2,0:T(8,128)(2,1)S(1)}, u32[]{:S(2)}, u32[]{:S(2)}) collective-permute-start(bf16[1,16,1,4,256]{4,1,3,2,0:T(8,128)(2,1)S(1)} %slice_bitcast_fusion.5), channel_id=1, source_target_pairs={{8,0},{16,8},{24,16},{32,24},{40,32},{48,40},{56,48},{64,56},{72,6... | collective-permute-start | bytes 98312 | tf_op jit(solution)/shard_map/ppermute | solution.py:25
  319.9 16.9 %collective-permute-start.10 = (bf16[1,16,10,1,256]{4,1,3,2,0:T(8,128)(2,1)S(1)}, bf16[1,16,10,1,256]{4,1,3,2,0:T(8,128)(2,1)S(1)}, u32[]{:S(2)}, u32[]{:S(2)}) collective-permute-start(bf16[1,16,10,1,256]{4,1,3,2,0:T(8,128)(2,1)S(1)} %get-tuple-element.19), channel_id=1, source_target_pairs={{0,1},{1,2},{2,3},{3,4},{4,5},{5,6},{6,7},{8,9},{9,10},{10,11},{11... | collective-permute-start | bytes 245768 | tf_op jit(solution)/shard_map/ppermute | solution.py:24
  324.4 12.4 %collective-permute-start.11 = (bf16[1,16,10,1,256]{4,1,3,2,0:T(8,128)(2,1)S(1)}, bf16[1,16,10,1,256]{4,1,3,2,0:T(8,128)(2,1)}, u32[]{:S(2)}, u32[]{:S(2)}) collective-permute-start(bf16[1,16,10,1,256]{4,1,3,2,0:T(8,128)(2,1)S(1)} %get-tuple-element.20), channel_id=1, source_target_pairs={{1,0},{2,1},{3,2},{4,3},{5,4},{6,5},{7,6},{9,8},{10,9},{11,10},{12... | collective-permute-start | bytes 245768 | tf_op jit(solution)/shard_map/ppermute | solution.py:25
  330.3 3.5 copy-start.3
  368.1 58.1 %all-to-all-start.8 = ((f32[32,1,2048]{2,1,0:T(1,128)}), f32[32,1,2048]{2,1,0:T(1,128)S(1)}, u32[]{:S(2)}, u32[]{:S(2)}) async-start(f32[32,1,2048]{2,1,0:T(1,128)} %reshape.443), calls=%async_computation.8 | async-start | bytes 524288 | tf_op jit(solution)/shard_map/all_to_all | solution.py:52
  420.4 61.1 %collective-permute-start.14 = (bf16[1,16,10,1,256]{4,1,3,2,0:T(8,128)(2,1)}, bf16[1,16,10,1,256]{4,1,3,2,0:T(8,128)(2,1)}, u32[]{:S(2)}, u32[]{:S(2)}) collective-permute-start(bf16[1,16,10,1,256]{4,1,3,2,0:T(8,128)(2,1)} %get-tuple-element.15), channel_id=1, source_target_pairs={{0,1},{1,2},{2,3},{3,4},{4,5},{5,6},{6,7},{8,9},{9,10},{10,11},{11... | collective-permute-start | bytes 245768 | tf_op jit(solution)/shard_map/ppermute | solution.py:24
  424.3 57.2 %collective-permute-start.15 = (bf16[1,16,10,1,256]{4,1,3,2,0:T(8,128)(2,1)}, bf16[1,16,10,1,256]{4,1,3,2,0:T(8,128)(2,1)}, u32[]{:S(2)}, u32[]{:S(2)}) collective-permute-start(bf16[1,16,10,1,256]{4,1,3,2,0:T(8,128)(2,1)} %get-tuple-element.16), channel_id=1, source_target_pairs={{1,0},{2,1},{3,2},{4,3},{5,4},{6,5},{7,6},{9,8},{10,9},{11,10},{12... | collective-permute-start | bytes 245768 | tf_op jit(solution)/shard_map/ppermute | solution.py:25
  433.9 24.7 %copy-start.5 = (bf16[8,4,8,33,16]{4,2,3,1,0:T(8,128)(2,1)S(1)}, bf16[8,4,8,33,16]{4,2,3,1,0:T(8,128)(2,1)}, u32[]{:S(2)}) copy-start(bf16[8,4,8,33,16]{4,2,3,1,0:T(8,128)(2,1)} %multiply_convert_fusion) | copy-start | bytes 811012
  446.3 48.2 %all-to-all-start.9 = ((f32[32,1,2048]{2,1,0:T(1,128)}), f32[32,1,2048]{2,1,0:T(1,128)S(1)}, u32[]{:S(2)}, u32[]{:S(2)}) async-start(f32[32,1,2048]{2,1,0:T(1,128)} %reshape.445), calls=%async_computation.9 | async-start | bytes 524288 | tf_op jit(solution)/shard_map/all_to_all | solution.py:56
  498.2 347.3 %all-to-all-start.10 = ((f32[2,4,8,1024]{3,1,0,2:T(4,128)}), f32[2,4,8,1024]{3,1,0,2:T(4,128)S(1)}, u32[]{:S(2)}, u32[]{:S(2)}) async-start(f32[2,4,8,1024]{3,1,0,2:T(4,128)} %reshape.426), calls=%async_computation.10 | async-start | bytes 524288 | tf_op jit(solution)/shard_map/all_to_all | solution.py:55
  503.7 90.1 %copy-start.11 = (f32[16,8,3,3,3]{0,1,4,3,2:T(8,128)S(1)}, f32[16,8,3,3,3]{0,1,4,3,2:T(8,128)}, u32[]{:S(2)}) copy-start(f32[16,8,3,3,3]{0,1,4,3,2:T(8,128)} %fusion.52) | copy-start | bytes 41476
  503.7 342.1 %copy-start.9 = (f32[1,2,32,32]{3,2,1,0:T(8,128)S(1)}, f32[1,2,32,32]{3,2,1,0:T(8,128)}, u32[]{:S(2)}) copy-start(f32[1,2,32,32]{3,2,1,0:T(8,128)} %get-tuple-element.33) | copy-start | bytes 24580
  503.7 342.1 %copy-start.10 = (f32[1,2,32,32]{3,2,1,0:T(8,128)S(1)}, f32[1,2,32,32]{3,2,1,0:T(8,128)}, u32[]{:S(2)}) copy-start(f32[1,2,32,32]{3,2,1,0:T(8,128)} %get-tuple-element.34) | copy-start | bytes 24580
  860.5 13.3 %all-to-all-start.11 = ((bf16[8,2,4096]{2,1,0:T(2,128)(2,1)}), bf16[8,2,4096]{2,1,0:T(2,128)(2,1)S(1)}, u32[]{:S(2)}, u32[]{:S(2)}) async-start(bf16[8,2,4096]{2,1,0:T(2,128)(2,1)} %reshape.447), calls=%async_computation.11 | async-start | bytes 262144 | tf_op jit(solution)/shard_map/all_to_all | solution.py:67
  867.9 26.4 %copy-start.1 = (bf16[16,8,3,3,3]{0,1,4,3,2:T(8,128)(2,1)S(1)}, bf16[16,8,3,3,3]{0,1,4,3,2:T(8,128)(2,1)}, u32[]{:S(2)}) copy-start(bf16[16,8,3,3,3]{0,1,4,3,2:T(8,128)(2,1)} %param.8) | copy-start | bytes 20740
  868.6 24.8 %copy-start.7 = (f32[2,4,8,4,256]{4,3,2,1,0:T(4,128)S(1)}, f32[2,4,8,4,256]{4,3,2,1,0:T(4,128)}, u32[]{:S(2)}) copy-start(f32[2,4,8,4,256]{4,3,2,1,0:T(4,128)} %param.7) | copy-start | bytes 786436
  868.6 24.9 %copy-start.12 = (f32[8,4]{1,0:T(8,128)S(1)}, f32[8,4]{1,0:T(8,128)}, u32[]{:S(2)}) copy-start(f32[8,4]{1,0:T(8,128)} %copy.333) | copy-start | bytes 388
